TPU v7x, 32 devices: a whole 2x2x4 slice. The times are simulated.
32 devices in a mesh: dp: 4 (over y, x), expert: 4 (over z), tensor: 2 (over core).
Axes of the slice: x: 2, y: 2, z: 4, core: 2. Of those that a mesh axis runs over, the one named last changes fastest.
Arguments:
- tokens: bfloat16 [8192, 1536], P(('dp', 'expert')), may hold values from -6 to 6
- out_grad: bfloat16 [8192, 1536], P(('dp', 'expert')), may hold values from -6 to 6
- attn_gain: float32 [1536], replicated, may hold values from 0.5 to 1.5
- query_weight: bfloat16 [1536, 1536], P(None, 'tensor'), may hold values from -0.625 to 0.625
- key_value_weight: bfloat16 [2, 1536, 512], P(None, None, 'tensor'), may hold values from -0.625 to 0.625
- output_weight: bfloat16 [1536, 1536], P('tensor'), may hold values from -0.625 to 0.625
- expert_gain: float32 [1536], replicated, may hold values from 0.5 to 1.5
- router_weight: bfloat16 [1536, 20], replicated, may hold values from -0.078125 to 0.078125
- gateup_weight: bfloat16 [20, 2, 1536, 512], P('expert', None, None, 'tensor'), may hold values from -0.15625 to 0.15625
- down_weight: bfloat16 [20, 512, 1536], P('expert', 'tensor'), may hold values from -4 to 4
- routes: int32 [8192, 8], P(('dp', 'expert')), may hold values from 0 to 19, all different within a row; in each aligned block of 512 rows (0 to 511, 512 to 1023, ...) at most 256 rows name the same one
Outputs:
- mixed: bfloat16 [8192, 1536], P(('dp', 'expert'))
- tokens_grad: float32 [8192, 1536], P(('dp', 'expert'))
- attn_gain_grad: float32 [1536], P(('dp', 'expert'))
- query_grad: float32 [1536, 1536], P(('dp', 'expert'), 'tensor')
- keyvalue_grad: float32 [2, 1536, 512], P(None, ('dp', 'expert'), 'tensor')
- output_weight_grad: float32 [1536, 1536], P('tensor', ('dp', 'expert'))
- expert_gain_grad: float32 [1536], P(('dp', 'expert'))
- router_grad: float32 [1536, 20], P(('dp', 'expert'))
- gateup_grad: float32 [20, 2, 1536, 512], P('expert', None, 'dp', 'tensor')
- down_grad: float32 [20, 512, 1536], P('expert', 'tensor', 'dp')
Inputs may be any that keep to these rules, and one draw needn't show every extreme that they name: `routes`: each row names 8 different experts. Within each aligned block of 512 rows no expert is named by more than 256 rows, a bound that some block reaches.
All inputs are finite; a program needn't handle non-finite values.
Results may differ from a plain program's by a relative error of at most 0.018.
The roundings to bfloat16 on the way count: a program that leaves them out, or rounds other values in their place, can miss the bound.
Values may be sent and summed in bfloat16 or wider, within the bound.
A program may use at most 320 MiB of HBM per device.

v0:
```python
import functools

import jax
import jax.numpy as jnp
import numpy as np
from jax import lax
from jax.experimental import pallas as pl
from jax.experimental.pallas import tpu as pltpu
from jax.sharding import PartitionSpec as P

HEAD_SIZE = 64
TOPK = 8
SEQUENCE_LENGTH = 512


EPSILON = 1e-06
RESIDUAL = 0.22
ATTN_SCALE = 0.015625
ROPE_BASE = 10000.0
NEGATIVE = -1e30
COT_STEPS = {1: (2,)}
EARLY = 2


def rotary_tables():
    half_dim = HEAD_SIZE // 2
    frequency = ROPE_BASE ** (-np.arange(half_dim, dtype=np.float32) * 2.0 / HEAD_SIZE)
    angles = np.arange(SEQUENCE_LENGTH, dtype=np.float32)[:, None] * frequency[None, :]
    angles = angles.astype(np.float32)
    cosine, sine = np.cos(angles), np.sin(angles)
    return (
        jnp.asarray(np.concatenate([cosine, cosine], axis=1), jnp.float32),
        jnp.asarray(np.concatenate([sine, -sine], axis=1), jnp.float32),
    )


def norm_parts(values):
    inv_rms = lax.rsqrt(jnp.mean(values * values, axis=-1, keepdims=True) + EPSILON)
    return values * inv_rms, inv_rms


def factors(count):
    low = 1 << ((count.bit_length() - 1) // 2)
    return count // low, low


class Place:
    def __init__(self, rows, columns, owners):
        self.sizes = {"y": rows, "x": columns, "z": owners}
        index = lax.axis_index("dp")
        self.at = {"y": index // columns, "x": index % columns, "z": lax.axis_index("expert")}

    def peer(self, axis, shift):
        return lax.rem(self.at[axis] + shift, self.sizes[axis])

    def device(self, axis, to):
        if axis == "z":
            return {"expert": to}
        if axis == "x":
            return {"dp": self.at["y"] * self.sizes["x"] + to}
        return {"dp": to * self.sizes["x"] + self.at["x"]}


def picked(ref, position, index):
    return ref.at[(slice(None),) * position + (index,)]


def contract(left, right, left_dim, right_dim):
    return lax.dot_general(
        left, right, (((left_dim,), (right_dim,)), ((), ())), preferred_element_type=jnp.float32
    )


def block_order(me, count, turn):
    block, unit = 0, 1
    while unit < count:
        block = block + unit * ((me // unit + turn // unit) % 2)
        unit *= 2
    return block


def expert_kernel(
    rows,
    columns,
    owners,
    local,
    early,
    tokens_hbm,
    cot_hbm,
    routes_ref,
    gains_ref,
    cosine_ref,
    sine_ref,
    router_ref,
    query_weight_hbm,
    keyvalue_weight_hbm,
    out_weight_hbm,
    gateup_hbm,
    down_hbm,
    parts_hbm,
    dots_hbm,
    comb_hbm,
    gates_out,
    grads_hbm,
    early_a,
    early_b,
    act_hbm,
    hidden_hbm,
    normed_hbm,
    query_hbm,
    key_hbm,
    value_hbm,
    heads_hbm,
    middle_hbm,
    rows_all,
    cot_all,
    hits_all,
    gateup_ref,
    down_ref,
    router_wide,
    half_send,
    half_land,
    gates_ref,
    send_grad,
    send_comb,
    send_dots,
    recv_grad,
    recv_comb,
    recv_dots,
    relay,
    load_sem,
    keep_sem,
    half_sem,
    weight_sem,
    chain_send,
    chain_recv,
    swap_send,
    swap_recv,
    sums_send,
    grad_recv,
    comb_recv,
    dots_recv,
    back_send,
    back_recv,
    dots_send,
    dots_back,
    hits_send,
    hits_recv,
    relay_sem,
    comb_sem,
    stage_sem,
    early_send,
    early_recv,
    dots_sem,
    grads_sem,
):
    place = Place(rows, columns, owners)
    me = lax.axis_index("expert")
    core = lax.axis_index("tensor")
    sibling = {"tensor": 1 - core}
    total, feat_width = rows_all.shape[1], rows_all.shape[2]
    half = total // 2
    units = down_ref.shape[0] // local
    lanes = gates_ref.shape[1]
    mine = pl.ds(pl.multiple_of(core * half, half), half)
    others = pl.ds(pl.multiple_of((1 - core) * half, half), half)

    barrier = pltpu.get_barrier_semaphore()
    pl.semaphore_signal(barrier, inc=1, device_id=sibling, device_id_type=pl.DeviceIdType.MESH)
    peers = 1
    for axis in ("x", "y", "z"):
        for shift in range(1, place.sizes[axis]):
            pl.semaphore_signal(
                barrier,
                inc=1,
                device_id=place.device(axis, place.peer(axis, shift)),
                device_id_type=pl.DeviceIdType.MESH,
            )
            peers += 1

    def remote(src, dst, send, recv, device):
        return pltpu.make_async_remote_copy(
            src_ref=src,
            dst_ref=dst,
            send_sem=send,
            recv_sem=recv,
            device_id=device,
            device_id_type=pl.DeviceIdType.MESH,
        )

    own_cot = pltpu.make_async_copy(cot_hbm, cot_all.at[me], load_sem.at[0])
    own_cot.start()
    number_of = lax.broadcasted_iota(jnp.int32, (lanes, total), 0)
    hits = number_of == routes_ref[0:1]
    for pick in range(1, routes_ref.shape[0]):
        hits = hits | (number_of == routes_ref[pick : pick + 1])
    hits_all[me] = jnp.where(hits, 1.0, 0.0).astype(jnp.bfloat16)
    experts_named = router_ref.shape[0]
    router_wide[...] = jnp.concatenate(
        [
            router_ref[...].astype(jnp.float32),
            jnp.zeros((lanes - experts_named, feat_width), jnp.float32),
        ],
        axis=0,
    ).astype(jnp.bfloat16)

    buffers = (rows_all, cot_all)

    def hits_copy(shift):
        return remote(
            hits_all.at[me],
            hits_all.at[me],
            hits_send.at[shift - 1],
            hits_recv.at[me],
            place.device("z", place.peer("z", shift)),
        )

    def hits_arrival(block):
        return remote(
            hits_all.at[block],
            hits_all.at[block],
            hits_send.at[0],
            hits_recv.at[block],
            sibling,
        )

    def chain(step, what, side):
        block = me - side * (step - 1)
        to = me + side
        there = (block >= 0) & (block < owners) & (to >= 0) & (to < owners)
        safe = jnp.clip(block, 0, owners - 1)
        at = 0 if side == 1 else 1
        copy = remote(
            buffers[what].at[safe, mine],
            buffers[what].at[safe, mine],
            chain_send.at[what, step - 1, at],
            chain_recv.at[what, safe],
            {"expert": jnp.clip(to, 0, owners - 1)},
        )
        return there, copy

    def swap(what, block):
        return remote(
            buffers[what].at[block, mine],
            buffers[what].at[block, mine],
            swap_send.at[what, block],
            swap_recv.at[what, block],
            sibling,
        )

    def swap_arrival(what, block):
        return remote(
            buffers[what].at[block, others],
            buffers[what].at[block, others],
            swap_send.at[what, block],
            swap_recv.at[what, block],
            sibling,
        )

    def send_step(step, what):
        for side in (1, -1):
            there, copy = chain(step, what, side)

            @pl.when(there)
            def _():
                copy.start()

    def arrivals(step, what):
        for side in (1, -1):
            block = me - side * step
            there = (block >= 0) & (block < owners)
            safe = jnp.clip(block, 0, owners - 1)

            @pl.when(there)
            def _():
                chain_copy = remote(
                    buffers[what].at[safe, mine],
                    buffers[what].at[safe, mine],
                    chain_send.at[what, step - 1, 0],
                    chain_recv.at[what, safe],
                    sibling,
                )
                chain_copy.wait_recv()

        if step + 1 < owners:
            send_step(step + 1, what)
        for side in (1, -1):
            block = me - side * step
            there = (block >= 0) & (block < owners)
            safe = jnp.clip(block, 0, owners - 1)

            @pl.when(there)
            def _():
                swap(what, safe).start()

    heads, length, head_size = query_hbm.shape
    kv_heads = key_hbm.shape[0]
    groups = heads // kv_heads
    tile = 64

    def part_of(expert, part):
        return pl.ds(pl.multiple_of((2 * expert + part) * units, units), units)

    def both_of(expert):
        return pl.ds(pl.multiple_of(2 * expert * units, 2 * units), 2 * units)

    def own_of(expert):
        return pl.ds(pl.multiple_of(expert * units, units), units)

    def weight_loads(expert):
        return [
            pltpu.make_async_copy(
                gateup_hbm.at[expert, part],
                gateup_ref.at[:, part_of(expert, part)],
                weight_sem.at[part, expert],
            )
            for part in range(2)
        ] + [
            pltpu.make_async_copy(
                down_hbm.at[expert], down_ref.at[own_of(expert)], weight_sem.at[2, expert]
            )
        ]

    def attention_phase(
        tokens, query_weight, keyvalue_weight, out_weight, normed, query, key, value, group_out, heads_out, partial, middle
    ):
        load_tokens = pltpu.make_async_copy(tokens_hbm, tokens, load_sem.at[1])
        loads = (
            pltpu.make_async_copy(query_weight_hbm, query_weight, load_sem.at[2]),
            pltpu.make_async_copy(keyvalue_weight_hbm, keyvalue_weight, load_sem.at[3]),
            pltpu.make_async_copy(out_weight_hbm, out_weight, load_sem.at[4]),
        )
        keeps = (
            pltpu.make_async_copy(normed, normed_hbm, keep_sem.at[0]),
            pltpu.make_async_copy(query, query_hbm, keep_sem.at[1]),
            pltpu.make_async_copy(key, key_hbm, keep_sem.at[2]),
            pltpu.make_async_copy(value, value_hbm, keep_sem.at[3]),
            pltpu.make_async_copy(heads_out, heads_hbm, keep_sem.at[4]),
            pltpu.make_async_copy(middle, middle_hbm, keep_sem.at[5]),
        )
        load_tokens.start()
        for copy in loads:
            copy.start()
        for expert in range(local):
            for copy in weight_loads(expert):
                copy.start()
        own_cot.wait()
        pl.semaphore_wait(barrier, peers)
        send_step(1, 1)
        for shift in range(1, owners):
            hits_copy(shift).start()
        load_tokens.wait()

        def first_norm(step, carry):
            at = pl.ds(pl.multiple_of(step * tile, tile), tile)
            unit, _ = norm_parts(tokens[at].astype(jnp.float32))
            normed[at] = (unit * gains_ref[0:1]).astype(jnp.bfloat16)
            return carry

        lax.fori_loop(0, total // tile, first_norm, 0)
        keeps[0].start()

        def turned(values):
            swapped = jnp.concatenate(
                [values[:, head_size // 2 :], values[:, : head_size // 2]], axis=1
            )
            return (values * cosine_ref[...] - swapped * sine_ref[...]).astype(jnp.bfloat16)

        loads[0].wait()
        projected = jnp.dot(normed[...], query_weight[...], preferred_element_type=jnp.float32)
        for head in range(heads):
            query[head] = turned(projected[:, head * head_size : (head + 1) * head_size])
        loads[1].wait()
        projected = jnp.dot(normed[...], keyvalue_weight[0], preferred_element_type=jnp.float32)
        for head in range(kv_heads):
            key[head] = turned(projected[:, head * head_size : (head + 1) * head_size])
        projected = jnp.dot(normed[...], keyvalue_weight[1], preferred_element_type=jnp.float32)
        for head in range(kv_heads):
            value[head] = projected[:, head * head_size : (head + 1) * head_size].astype(
                jnp.bfloat16
            )
        for copy in keeps[1:4]:
            copy.start()
        causal = length // 2

        def body(group, carry):
            keys, values = key[group], value[group]
            found = []
            for member in range(groups):
                some = query[group * groups + member]
                pieces = []
                for start in (0, causal):
                    stop = start + causal
                    scores = contract(some[start:stop], keys[:stop], 1, 1) * ATTN_SCALE
                    row = start + lax.broadcasted_iota(jnp.int32, scores.shape, 0)
                    col = lax.broadcasted_iota(jnp.int32, scores.shape, 1)
                    scores = jnp.where(row >= col, scores, NEGATIVE)
                    raised = jnp.exp(scores - jnp.max(scores, axis=1, keepdims=True))
                    probs = raised * (1.0 / jnp.sum(raised, axis=1, keepdims=True))
                    pieces.append(
                        jnp.dot(
                            probs.astype(jnp.bfloat16),
                            values[:stop],
                            preferred_element_type=jnp.float32,
                        )
                    )
                found.append(jnp.concatenate(pieces, axis=0))
            group_out[group] = jnp.concatenate(found, axis=1).astype(jnp.bfloat16)

            @pl.when(group == kv_heads - 1)
            def _():
                arrivals(1, 1)

            return carry

        lax.fori_loop(0, kv_heads, body, 0)
        heads_out[...] = jnp.concatenate([group_out[g] for g in range(kv_heads)], axis=1)
        keeps[4].start()
        loads[2].wait()
        half_send[...] = jnp.dot(
            heads_out[others], out_weight[...], preferred_element_type=jnp.float32
        ).astype(jnp.bfloat16)
        half_copy = remote(half_send, half_land, half_sem.at[0], half_sem.at[1], sibling)
        half_copy.start()
        partial[...] = jnp.dot(
            heads_out[mine], out_weight[...], preferred_element_type=jnp.float32
        )
        half_copy.wait()

        def second_norm(step, carry):
            at = pl.ds(pl.multiple_of(step * tile, tile), tile)
            to = pl.ds(pl.multiple_of(core * half + step * tile, tile), tile)
            after = tokens[to].astype(jnp.float32) + RESIDUAL * (
                partial[at] + half_land[at].astype(jnp.float32)
            )
            middle[at] = after
            unit, _ = norm_parts(after)
            rows_all[me, to] = (unit * gains_ref[1:2]).astype(jnp.bfloat16)
            return carry

        lax.fori_loop(0, half // tile, second_norm, 0)
        swap(0, me).start()
        send_step(1, 0)
        keeps[5].start()
        for copy in keeps:
            copy.wait()

    pl.run_scoped(
        attention_phase,
        pltpu.VMEM((total, feat_width), jnp.bfloat16),
        pltpu.VMEM(query_weight_hbm.shape, jnp.bfloat16),
        pltpu.VMEM(keyvalue_weight_hbm.shape, jnp.bfloat16),
        pltpu.VMEM(out_weight_hbm.shape, jnp.bfloat16),
        pltpu.VMEM((total, feat_width), jnp.bfloat16),
        pltpu.VMEM(query_hbm.shape, jnp.bfloat16),
        pltpu.VMEM(key_hbm.shape, jnp.bfloat16),
        pltpu.VMEM(value_hbm.shape, jnp.bfloat16),
        pltpu.VMEM((kv_heads, total, groups * head_size), jnp.bfloat16),
        pltpu.VMEM(heads_hbm.shape, jnp.bfloat16),
        pltpu.VMEM((half, feat_width), jnp.float32),
        pltpu.VMEM((half, feat_width), jnp.float32),
    )

    width = feat_width // (rows * columns)
    inside = min(early, 2)

    def term_loads(act, hidden, slot, expert, turns):
        some = pl.ds(turns[0], len(turns))
        return (
            pltpu.make_async_copy(act_hbm.at[expert, some], act.at[slot], dots_sem.at[0, slot]),
            pltpu.make_async_copy(
                hidden_hbm.at[expert, some], hidden.at[slot], dots_sem.at[1, slot]
            ),
        )

    def weight_grads(terms, grads):
        up_sum = sum(
            contract(rows_all[block_order(me, owners, turn)], hidden[...], 0, 0)
            for _, hidden, turn in terms
        ).astype(jnp.bfloat16)
        down_sum = sum(
            contract(act[...], cot_all[block_order(me, owners, turn)], 0, 0)
            for act, _, turn in terms
        )
        down_sum = (RESIDUAL * down_sum).T.astype(jnp.bfloat16)
        for y in range(rows):
            for x in range(columns):
                start = (y * columns + x) * width
                for part in range(2):
                    grads[y, x, part, :width] = up_sum[
                        start : start + width, part * units : (part + 1) * units
                    ]
                    at = start + part * (width // 2)
                    grads[y, x, part, width:] = down_sum[at : at + width // 2]

    def store_grads(grads, expert, slot):
        return pltpu.make_async_copy(grads, grads_hbm.at[:, :, expert], grads_sem.at[slot])

    def early_copies(grads, expert):
        found = []
        for part, axis, landing in ((0, "x", early_a), (1, "y", early_b)):
            for shift in range(1, place.sizes[axis]):
                to = place.peer(axis, shift)
                found.append(
                    remote(
                        grads.at[:, to, part] if axis == "x" else grads.at[to, :, part],
                        landing.at[shift - 1, expert],
                        early_send.at[part, shift - 1, expert],
                        early_recv.at[part, shift - 1, expert],
                        place.device(axis, to),
                    )
                )
        return found

    relays = owners == 4
    middle_owner = (me > 0) & (me < owners - 1)

    def goes_back(turn):
        if not relays:
            return turn > 0
        return ((turn != 1) & (turn != 2)) | ~middle_owner

    def back_copy(turn):
        return remote(
            recv_grad.at[turn],
            parts_hbm.at[turn],
            back_send.at[turn],
            back_recv.at[turn],
            {"expert": block_order(me, owners, turn)},
        )

    def dots_copy(turn):
        return remote(
            recv_dots.at[turn],
            dots_hbm.at[turn],
            dots_send.at[turn],
            dots_back.at[turn],
            {"expert": block_order(me, owners, turn)},
        )

    def relay_copy():
        return remote(
            recv_grad.at[2],
            relay,
            relay_sem.at[0],
            relay_sem.at[1],
            {"expert": block_order(me, owners, 3)},
        )

    def expert_phase(
        dot_sum, hold_comb, hold_grad, hold_dot, act_block, hidden_block, act_terms, hidden_terms, grads
    ):
        lane = lax.broadcasted_iota(jnp.int32, (total, lanes), 1)

        def stage_copies(expert, turn):
            return (
                pltpu.make_async_copy(
                    act_block.at[:, own_of(expert)],
                    act_hbm.at[expert, turn],
                    stage_sem.at[0, expert],
                ),
                pltpu.make_async_copy(
                    hidden_block.at[:, both_of(expert)],
                    hidden_hbm.at[expert, turn],
                    stage_sem.at[1, expert],
                ),
            )

        def sums_copies(turn):
            return (
                remote(send_grad, recv_grad.at[turn], sums_send.at[0], grad_recv.at[turn], sibling),
                remote(send_comb, recv_comb.at[turn], sums_send.at[1], comb_recv.at[turn], sibling),
                remote(send_dots, recv_dots.at[turn], sums_send.at[2], dots_recv.at[turn], sibling),
            )

        def own_back():
            return (
                pltpu.make_async_copy(recv_grad.at[0], parts_hbm.at[0], back_send.at[0]),
                pltpu.make_async_copy(recv_dots.at[0], dots_hbm.at[0], dots_send.at[0]),
            )

        def comb_copy(turn, block):
            return pltpu.make_async_copy(
                recv_comb.at[turn],
                comb_hbm.at[lax.rem(block - me + owners, owners)],
                comb_sem.at[turn],
            )

        def settle(turn):
            block = block_order(me, owners, turn)
            copy_grad, copy_comb, copy_dots = sums_copies(turn)
            copy_dots.wait_recv()
            recv_dots[turn] = hold_dot[...] + recv_dots[turn]
            copy_grad.wait_recv()
            recv_grad[turn] = (
                hold_grad[...] + recv_grad[turn].astype(jnp.float32)
            ).astype(jnp.bfloat16)

            @pl.when(turn > 0)
            def _():
                dots_copy(turn).start()

            @pl.when((turn > 0) & goes_back(turn))
            def _():
                back_copy(turn).start()

            if relays:

                @pl.when((turn == 2) & middle_owner)
                def _():
                    relay_copy().start()

            @pl.when(turn == 0)
            def _():
                for copy in own_back():
                    copy.start()

            copy_comb.wait_recv()
            recv_comb[turn] = (hold_comb[...] + recv_comb[turn].astype(jnp.float32)).astype(
                jnp.bfloat16
            )
            comb_copy(turn, block).start()

        last = (owners - 1) * local

        def body(number, carry):
            turn = number // local
            expert = number % local
            block = block_order(me, owners, turn)

            @pl.when(expert == 0)
            def _():
                swap_arrival_needed = turn > 0

                @pl.when(swap_arrival_needed)
                def _():
                    swap_arrival(1, block).wait_recv()
                    hits_arrival(block).wait_recv()

                swap_arrival(0, block).wait_recv()
                hits = hits_all[block].astype(jnp.float32).T > 0.5
                logits = contract(rows_all[block], router_wide[...], 1, 1)
                logits = jnp.where(hits, logits, NEGATIVE)
                raised = jnp.where(
                    hits, jnp.exp(logits - jnp.max(logits, axis=1, keepdims=True)), 0.0
                )
                gates_ref[...] = raised / jnp.sum(raised, axis=1, keepdims=True)

                @pl.when(turn == 0)
                def _():
                    gates_out[...] = gates_ref[mine]

            @pl.when(number < local)
            def _():
                for copy in weight_loads(expert):
                    copy.wait()

            @pl.when((turn > 0) & (number < last))
            def _():
                for copy in stage_copies(expert, turn):
                    copy.wait()

            chosen = rows_all[block]
            gate_part = jnp.dot(
                chosen, gateup_ref[:, part_of(expert, 0)], preferred_element_type=jnp.float32
            )
            up_part = jnp.dot(
                chosen, gateup_ref[:, part_of(expert, 1)], preferred_element_type=jnp.float32
            )
            raw = contract(cot_all[block], down_ref[own_of(expert)], 1, 1)
            here = lane == me * local + expert
            weight = jnp.sum(jnp.where(here, gates_ref[...], 0.0), axis=1, keepdims=True)
            sigmoid_gate = 0.5 * jnp.tanh(0.5 * gate_part) + 0.5
            silu_gate = gate_part * sigmoid_gate
            activation = silu_gate * up_part
            dots = jnp.where(here, jnp.sum(activation * raw, axis=1, keepdims=True), 0.0)
            weighted = (activation * weight).astype(jnp.bfloat16)
            act_block[:, own_of(expert)] = weighted
            grad_act = raw * (RESIDUAL * weight)
            grad_gatepart = (
                grad_act * up_part * (sigmoid_gate * (1.0 + gate_part * (1.0 - sigmoid_gate)))
            ).astype(jnp.bfloat16)
            grad_uppart = (grad_act * silu_gate).astype(jnp.bfloat16)
            hidden_block[:, part_of(expert, 0)] = grad_gatepart
            hidden_block[:, part_of(expert, 1)] = grad_uppart
            for copy in stage_copies(expert, turn):
                copy.start()

            @pl.when(expert == 0)
            def _():
                dot_sum[...] = dots

            @pl.when(expert > 0)
            def _():
                dot_sum[...] += dots

            @pl.when((expert == 1) & (turn > 0) & (turn < owners - 1))
            def _():
                settle(turn - 1)

            for step in range(1, owners - 1):

                @pl.when(number == step * local - 2)
                def _():
                    for late in COT_STEPS.get(step, ()):
                        arrivals(late, 1)
                    arrivals(step, 0)

            @pl.when(expert == local - 1)
            def _():
                @pl.when(turn > 0)
                def _():
                    for copy in sums_copies(turn):
                        copy.wait_send()

                def grad_of(some):
                    return contract(hidden_block[some], gateup_ref[...], 1, 1)

                def comb_of(some):
                    return jnp.dot(
                        act_block[some], down_ref[...], preferred_element_type=jnp.float32
                    )

                send_grad[...] = grad_of(others).astype(jnp.bfloat16)
                send_dots[...] = dot_sum[others].T
                send_comb[...] = comb_of(others).astype(jnp.bfloat16)
                for copy in sums_copies(turn):
                    copy.start()
                hold_grad[...] = grad_of(mine)
                hold_comb[...] = comb_of(mine)
                hold_dot[...] = dot_sum[mine].T

            return carry

        lax.fori_loop(0, last, body, 0)
        settle(owners - 2)
        for expert in range(local):
            for copy in stage_copies(expert, 0):
                copy.wait()
        earlier = range(owners - 1)
        for copy in term_loads(act_terms, hidden_terms, 0, 0, earlier):
            copy.start()
        for step in range(2, owners):
            if not any(step in late for late in COT_STEPS.values()):
                arrivals(step, 1)
        arrivals(owners - 1, 0)


        def with_weights(expert, carry):
            body(last + expert, carry)
            for copy in term_loads(act_terms, hidden_terms, 0, expert, earlier):
                copy.wait()
            terms = [
                (act_terms.at[0, turn], hidden_terms.at[0, turn], turn) for turn in earlier
            ] + [
                (
                    act_block.at[:, own_of(expert)],
                    hidden_block.at[:, both_of(expert)],
                    owners - 1,
                )
            ]
            weight_grads(terms, grads.at[expert % 2])
            store_grads(grads.at[expert % 2], expert, expert % 2).start()
            for copy in early_copies(grads.at[expert % 2], expert):
                copy.start()

            @pl.when(expert + 1 < inside)
            def _():
                for copy in term_loads(act_terms, hidden_terms, 0, expert + 1, earlier):
                    copy.start()

            return carry

        lax.fori_loop(0, inside, with_weights, 0)
        lax.fori_loop(last + inside, owners * local, body, 0)
        settle(owners - 1)
        if relays:

            @pl.when(middle_owner)
            def _():
                relay_copy().wait_recv()
                recv_grad[1] = (
                    recv_grad[1].astype(jnp.float32) + relay[...].astype(jnp.float32)
                ).astype(jnp.bfloat16)
                back_copy(1).start()

        for copy in sums_copies(owners - 1):
            copy.wait_send()
        for expert in range(local):
            for copy in stage_copies(expert, 0):
                copy.wait()
        for expert in range(inside):
            store_grads(grads.at[expert % 2], expert, expert % 2).wait()
            for copy in early_copies(grads.at[expert % 2], expert):
                copy.wait_send()
        for turn in range(owners):
            block = block_order(me, owners, turn)
            comb_copy(turn, block).wait()

    pl.run_scoped(
        expert_phase,
        pltpu.VMEM((total, lanes), jnp.float32),
        pltpu.VMEM((half, feat_width), jnp.float32),
        pltpu.VMEM((half, feat_width), jnp.float32),
        pltpu.VMEM((lanes, half), jnp.float32),
        pltpu.VMEM((total, local * units), jnp.bfloat16),
        pltpu.VMEM((total, 2 * local * units), jnp.bfloat16),
        pltpu.VMEM((1, owners - 1, total, units), jnp.bfloat16),
        pltpu.VMEM((1, owners - 1, total, 2 * units), jnp.bfloat16),
        pltpu.VMEM((2,) + grads_hbm.shape[:2] + grads_hbm.shape[3:], jnp.bfloat16),
    )

    def weights_phase(act, hidden, grads):
        turns = range(owners)

        def loads(expert):
            return term_loads(act, hidden, expert % 2, expert, turns)

        def sent(expert):
            store_grads(grads.at[expert % 2], expert, expert % 2).wait()

            @pl.when(expert < early)
            def _():
                for copy in early_copies(grads.at[expert % 2], expert):
                    copy.wait_send()

        for copy in loads(inside):
            copy.start()

        def body(expert, carry):
            slot = expert % 2

            @pl.when(expert + 1 < local)
            def _():
                for copy in loads(expert + 1):
                    copy.start()

            for copy in loads(expert):
                copy.wait()

            @pl.when(expert >= inside + 2)
            def _():
                sent(expert - 2)

            terms = [(act.at[slot, turn], hidden.at[slot, turn], turn) for turn in turns]
            weight_grads(terms, grads.at[slot])
            store_grads(grads.at[slot], expert, slot).start()

            @pl.when(expert < early)
            def _():
                for copy in early_copies(grads.at[slot], expert):
                    copy.start()

            return carry

        lax.fori_loop(inside, local, body, 0)
        for expert in range(max(inside, local - 2), local):
            sent(expert)

    pl.run_scoped(
        weights_phase,
        pltpu.VMEM((2, owners, total, units), jnp.bfloat16),
        pltpu.VMEM((2, owners, total, 2 * units), jnp.bfloat16),
        pltpu.VMEM((2,) + grads_hbm.shape[:2] + grads_hbm.shape[3:], jnp.bfloat16),
    )
    for expert in range(early):
        for copy in early_copies(grads_hbm.at[:, :, expert], expert):
            copy.wait_recv()

    swap(0, me).wait_send()
    for step in range(1, owners):
        for what in range(2):
            for side in (1, -1):
                there, copy = chain(step, what, side)

                @pl.when(there)
                def _():
                    copy.wait_send()

                block = me - side * step
                arrived = (block >= 0) & (block < owners)
                safe = jnp.clip(block, 0, owners - 1)

                @pl.when(arrived)
                def _():
                    swap(what, safe).wait_send()

    for shift in range(1, owners):
        hits_copy(shift).wait_send()
    pltpu.make_async_copy(recv_grad.at[0], parts_hbm.at[0], back_send.at[0]).wait()
    pltpu.make_async_copy(recv_dots.at[0], dots_hbm.at[0], dots_send.at[0]).wait()
    for turn in range(1, owners):
        dots_copy(turn).wait()
        if relays and turn == 1:
            back_copy(turn).wait()
        elif relays and turn == 2:

            @pl.when(middle_owner)
            def _():
                relay_copy().wait_send()
                back_copy(turn).wait_recv()

            @pl.when(~middle_owner)
            def _():
                back_copy(turn).wait_send()
                none = pltpu.make_async_copy(half_send, parts_hbm.at[turn], load_sem.at[0])
                half_send[...] = jnp.zeros_like(half_send)
                none.start()
                none.wait()

        else:
            back_copy(turn).wait()


def experts(
    tokens,
    cot,
    routes,
    gains,
    cosine,
    sine,
    router,
    query_weight,
    keyvalue_weight,
    out_weight,
    gateup,
    down,
):
    owners = lax.axis_size("expert")
    rows, columns = factors(lax.axis_size("dp"))
    total, feat_width = tokens.shape
    half = total // 2
    local, units = down.shape[0], down.shape[1]
    height = 3 * feat_width // (rows * columns) // 2
    early = min(EARLY, local)
    most = max(rows, columns) - 1
    lanes = 32
    heads = query_weight.shape[1] // HEAD_SIZE
    kv_heads = keyvalue_weight.shape[2] // HEAD_SIZE
    hbm = pl.BlockSpec(memory_space=pl.ANY)
    vmem = pl.BlockSpec(memory_space=pltpu.VMEM)
    bf16, f32 = jnp.bfloat16, jnp.float32
    dma = pltpu.SemaphoreType.DMA
    return pl.pallas_call(
        functools.partial(expert_kernel, rows, columns, owners, local, early),
        in_specs=[hbm, hbm] + [vmem] * 5 + [hbm] * 5,
        out_specs=[hbm, hbm, hbm, vmem] + [hbm] * 11,
        out_shape=[
            jax.ShapeDtypeStruct((owners, half, feat_width), bf16),
            jax.ShapeDtypeStruct((owners, lanes, half), f32),
            jax.ShapeDtypeStruct((owners, half, feat_width), bf16),
            jax.ShapeDtypeStruct((half, lanes), f32),
            jax.ShapeDtypeStruct((rows, columns, local, 2, height, units), bf16),
            jax.ShapeDtypeStruct((columns - 1, early, rows, height, units), bf16),
            jax.ShapeDtypeStruct((rows - 1, early, columns, height, units), bf16),
            jax.ShapeDtypeStruct((local, owners, total, units), bf16),
            jax.ShapeDtypeStruct((local, owners, total, 2 * units), bf16),
            jax.ShapeDtypeStruct((total, feat_width), bf16),
            jax.ShapeDtypeStruct((heads, total, HEAD_SIZE), bf16),
            jax.ShapeDtypeStruct((kv_heads, total, HEAD_SIZE), bf16),
            jax.ShapeDtypeStruct((kv_heads, total, HEAD_SIZE), bf16),
            jax.ShapeDtypeStruct((total, heads * HEAD_SIZE), bf16),
            jax.ShapeDtypeStruct((half, feat_width), f32),
        ],
        scratch_shapes=[
            pltpu.VMEM((owners, total, feat_width), bf16),
            pltpu.VMEM((owners, total, feat_width), bf16),
            pltpu.VMEM((owners, lanes, total), bf16),
            pltpu.VMEM((feat_width, 2 * local * units), bf16),
            pltpu.VMEM((local * units, feat_width), bf16),
            pltpu.VMEM((lanes, feat_width), bf16),
            pltpu.VMEM((half, feat_width), bf16),
            pltpu.VMEM((half, feat_width), bf16),
            pltpu.VMEM((total, lanes), f32),
            pltpu.VMEM((half, feat_width), bf16),
            pltpu.VMEM((half, feat_width), bf16),
            pltpu.VMEM((lanes, half), f32),
            pltpu.VMEM((owners, half, feat_width), bf16),
            pltpu.VMEM((owners, half, feat_width), bf16),
            pltpu.VMEM((owners, lanes, half), f32),
            pltpu.VMEM((half, feat_width), bf16),
            dma((5,)),
            dma((6,)),
            dma((2,)),
            dma((3, local)),
            dma((2, owners - 1, 2)),
            dma((2, owners)),
            dma((2, owners)),
            dma((2, owners)),
            dma((3,)),
            dma((owners,)),
            dma((owners,)),
            dma((owners,)),
            dma((owners,)),
            dma((owners,)),
            dma((owners,)),
            dma((owners,)),
            dma((owners - 1,)),
            dma((owners,)),
            dma((2,)),
            dma((owners,)),
            dma((2, local)),
            dma((2, most, early)),
            dma((2, most, early)),
            dma((2, 2)),
            dma((2,)),
        ],
        compiler_params=pltpu.CompilerParams(
            vmem_limit_bytes=60 * 2**20, collective_id=0, has_side_effects=True
        ),
        cost_estimate=pl.CostEstimate(
            flops=2 * owners * total * feat_width * units * 9 * local,
            bytes_accessed=80 * 2**20,
            transcendentals=owners * total * units * local,
        ),
    )(
        tokens,
        cot,
        routes,
        gains,
        cosine,
        sine,
        router,
        query_weight,
        keyvalue_weight,
        out_weight,
        gateup,
        down,
    )


class Summing:
    def __init__(self, place, source, axes, order, landing, send, recv):
        self.place, self.order, self.landing = place, order, landing
        self.send, self.recv = send, recv
        self.sources, self.positions = [source], []
        left = list(axes)
        for step, axis in enumerate(order):
            self.positions.append(left.index(axis))
            left.pop(self.positions[-1])
            self.sources.append(landing[step].at[0])

    def copies(self, step):
        axis = self.order[step]
        found = []
        for shift in range(1, self.place.sizes[axis]):
            to = self.place.peer(axis, shift)
            found.append(
                pltpu.make_async_remote_copy(
                    src_ref=picked(self.sources[step], self.positions[step], to),
                    dst_ref=self.landing[step].at[shift - 1],
                    send_sem=self.send.at[step, shift - 1],
                    recv_sem=self.recv.at[step, shift - 1],
                    device_id=self.place.device(axis, to),
                    device_id_type=pl.DeviceIdType.MESH,
                )
            )
        return found

    def start(self, step):
        for copy in self.copies(step):
            copy.start()

    def total(self, step):
        axis = self.order[step]
        for copy in self.copies(step):
            copy.wait_recv()
        own = picked(self.sources[step], self.positions[step], self.place.at[axis])
        value = own[...].astype(jnp.float32)
        for shift in range(1, self.place.sizes[axis]):
            value = value + self.landing[step][shift - 1].astype(jnp.float32)
        return value

    def forward(self, step):
        self.landing[step][0] = self.total(step).astype(self.landing[step].dtype)
        self.start(step + 1)

    def close(self):
        for step in range(len(self.order)):
            for copy in self.copies(step):
                copy.wait_send()


def norm_grad(grad, gain, unit, inv_rms):
    grad_unit = grad * gain
    return inv_rms * (grad_unit - unit * jnp.mean(grad_unit * unit, axis=-1, keepdims=True))


def back_kernel(
    rows,
    columns,
    owners,
    parts_hbm,
    dots_hbm,
    comb_hbm,
    grads_hbm,
    early_a,
    early_b,
    gates_ref,
    middle_hbm,
    cot_hbm,
    tokens_hbm,
    gains_ref,
    router_ref,
    out_weight_hbm,
    heads_hbm,
    query_hbm,
    key_hbm,
    value_hbm,
    normed_hbm,
    query_weight_hbm,
    keyvalue_weight_hbm,
    cosine_ref,
    sine_ref,
    mixed_hbm,
    tokens_grad_hbm,
    kept_hbm,
    second_a,
    second_b,
    query_out,
    keyvalue_out,
    output_out,
    router_out,
    expert_gain_out,
    attn_gain_out,
    own_a,
    own_b,
    first_a,
    first_b,
    comb_own,
    comb_left,
    comb_right,
    out_a,
    out_az,
    out_ax,
    out_ay,
    out_b,
    out_by,
    out_bx,
    out_bz,
    near_q,
    near_qx,
    near_qy,
    near_qz,
    near_kv,
    near_kvy,
    near_kvx,
    near_kvz,
    far_q,
    far_qy,
    far_qx,
    far_qz,
    far_kv,
    far_kvx,
    far_kvy,
    far_kvz,
    small_sum,
    small_swap,
    small_stage,
    small_z,
    small_x,
    small_y,
    grad_attn,
    grad_middle,
    grad_query,
    grad_keyvalue,
    half_send,
    half_land,
    mixed_stage,
    load_sem,
    own_sem,
    keep_sem,
    early_sem,
    first_send,
    first_recv,
    second_send,
    second_recv,
    comb_sem,
    comb_send,
    comb_recv,
    sum_send,
    sum_recv,
    swap_send,
    swap_recv,
    store_sem,
):
    place = Place(rows, columns, owners)
    core = lax.axis_index("tensor")
    sibling = {"tensor": 1 - core}
    half, feat_width = middle_hbm.shape
    local = grads_hbm.shape[2]
    early = early_a.shape[1]
    heads, length, head_size = query_hbm.shape
    kv_heads = key_hbm.shape[0]
    groups = heads // kv_heads
    query_width = heads * head_size
    key_width = kv_heads * head_size
    tile = 64
    mine = pl.ds(pl.multiple_of(core * half, half), half)
    others = pl.ds(pl.multiple_of((1 - core) * half, half), half)

    barrier = pltpu.get_barrier_semaphore()
    peers = [sibling]
    for axis in ("x", "y", "z"):
        for shift in range(1, place.sizes[axis]):
            peers.append(place.device(axis, place.peer(axis, shift)))
    for peer in peers:
        pl.semaphore_signal(barrier, inc=1, device_id=peer, device_id_type=pl.DeviceIdType.MESH)
    pl.semaphore_wait(barrier, len(peers))

    def to_sibling(src, dst, at):
        return pltpu.make_async_remote_copy(
            src_ref=src,
            dst_ref=dst,
            send_sem=swap_send.at[at],
            recv_sem=swap_recv.at[at],
            device_id=sibling,
            device_id_type=pl.DeviceIdType.MESH,
        )

    plans = (
        (0, "x", "y", own_a, first_a, second_a),
        (1, "y", "x", own_b, first_b, second_b),
    )

    def grads_of(part, axis, index, expert):
        if axis == "x":
            return grads_hbm.at[:, index, expert, part]
        return grads_hbm.at[index, :, expert, part]

    def own_load(plan, expert):
        part, axis, _, own, _, _ = plan
        return pltpu.make_async_copy(
            grads_of(part, axis, place.at[axis], expert),
            own.at[expert % 2],
            own_sem.at[part, expert],
        )

    def early_load(plan, expert):
        part, _, _, _, first, _ = plan
        source = (early_a, early_b)[part]
        return pltpu.make_async_copy(
            source.at[:, expert], first.at[:, expert], early_sem.at[part, expert]
        )

    def first_copies(plan, expert):
        part, axis, _, _, first, _ = plan
        found = []
        for shift in range(1, place.sizes[axis]):
            to = place.peer(axis, shift)
            found.append(
                pltpu.make_async_remote_copy(
                    src_ref=grads_of(part, axis, to, expert),
                    dst_ref=first.at[shift - 1, expert],
                    send_sem=first_send.at[part, shift - 1, expert],
                    recv_sem=first_recv.at[part, shift - 1, expert],
                    device_id=place.device(axis, to),
                    device_id_type=pl.DeviceIdType.MESH,
                )
            )
        return found

    def second_copies(plan, expert):
        part, _, axis, _, first, second = plan
        found = []
        for shift in range(1, place.sizes[axis]):
            to = place.peer(axis, shift)
            found.append(
                pltpu.make_async_remote_copy(
                    src_ref=first.at[0, expert, to],
                    dst_ref=second.at[shift - 1, expert],
                    send_sem=second_send.at[part, shift - 1, expert],
                    recv_sem=second_recv.at[part, shift - 1, expert],
                    device_id=place.device(axis, to),
                    device_id_type=pl.DeviceIdType.MESH,
                )
            )
        return found

    def first_sum(expert):
        for plan in plans:
            _, axis, after, own, first, _ = plan
            own_load(plan, expert).wait()

            @pl.when(expert < early)
            def _():
                early_load(plan, expert).wait()

            @pl.when(expert >= early)
            def _():
                for copy in first_copies(plan, expert):
                    copy.wait_recv()

            for index in range(place.sizes[after]):
                value = own[expert % 2, index].astype(jnp.float32)
                for shift in range(1, place.sizes[axis]):
                    value = value + first[shift - 1, expert, index].astype(jnp.float32)
                first[0, expert, index] = value.astype(first.dtype)

            @pl.when(expert + 2 < local)
            def _():
                own_load(plan, expert + 2).start()

    def keep(plan, expert):
        part, _, axis, _, first, _ = plan
        return pltpu.make_async_copy(
            first.at[0, expert, place.at[axis]],
            kept_hbm.at[part, expert],
            keep_sem.at[part, expert],
        )

    def start_first(expert, carry):
        for plan in plans:
            for copy in first_copies(plan, expert):
                copy.start()
        return carry

    held = local - 1
    lax.fori_loop(early, held, start_first, 0)
    for plan in plans:
        for expert in range(early):
            early_load(plan, expert).start()
        for expert in range(min(2, local)):
            own_load(plan, expert).start()

    me = place.at["z"]

    def comb_load(shift):
        return pltpu.make_async_copy(comb_hbm.at[shift], comb_own.at[shift], comb_sem.at[shift])

    def comb_copy(side, away):
        landing, at = (comb_right, 0) if side == 1 else (comb_left, 1)
        shift = away if side == 1 else owners - away
        to = jnp.clip(me + side, 0, owners - 1)
        return pltpu.make_async_remote_copy(
            src_ref=comb_own.at[shift],
            dst_ref=landing.at[away - 1],
            send_sem=comb_send.at[at, away],
            recv_sem=comb_recv.at[at, away - 1],
            device_id=place.device("z", to),
            device_id_type=pl.DeviceIdType.MESH,
        )

    def comb_arrival(side, away):
        landing, at = (comb_right, 0) if side == 1 else (comb_left, 1)
        from_ = jnp.clip(me - side, 0, owners - 1)
        return pltpu.make_async_remote_copy(
            src_ref=comb_own.at[0],
            dst_ref=landing.at[away],
            send_sem=comb_send.at[at, away],
            recv_sem=comb_recv.at[at, away],
            device_id=place.device("z", from_),
            device_id_type=pl.DeviceIdType.MESH,
        )

    def inside(at):
        return (at >= 0) & (at < owners)

    def comb_send_on(away):
        for side in (1, -1):

            @pl.when(inside(me + side * away))
            def _():
                comb_copy(side, away).start()

    def comb_add(away):
        for side in (1, -1):

            @pl.when(inside(me + side * away) & inside(me - side))
            def _():
                comb_arrival(side, away).wait_recv()
                landing = comb_right if side == 1 else comb_left
                shift = 0 if away == 0 else (away if side == 1 else owners - away)
                comb_own[shift] = (
                    comb_own[shift].astype(jnp.float32) + landing[away].astype(jnp.float32)
                ).astype(jnp.bfloat16)

    def comb_stage(away):
        comb_add(away)
        if away > 0:
            comb_send_on(away)

    def job(source, order, landing, at):
        return Summing(
            place, source, ("y", "x", "z"), order, landing, sum_send.at[at], sum_recv.at[at]
        )

    output_job_a = job(out_a, ("z", "x", "y"), (out_az, out_ax, out_ay), 0)
    output_job_b = job(out_b, ("y", "x", "z"), (out_by, out_bx, out_bz), 4)
    pair_jobs = (
        (
            job(near_q, ("x", "y", "z"), (near_qx, near_qy, near_qz), 1),
            job(near_kv, ("y", "x", "z"), (near_kvy, near_kvx, near_kvz), 2),
        ),
        (
            job(far_q, ("y", "x", "z"), (far_qy, far_qx, far_qz), 5),
            job(far_kv, ("x", "y", "z"), (far_kvx, far_kvy, far_kvz), 6),
        ),
    )
    pair_stages = ((near_q, near_kv), (far_q, far_kv))
    small_job = job(small_stage, ("z", "x", "y"), (small_z, small_x, small_y), 3)

    def weight_grad(stage, left, right):
        count = stage.shape[3]
        band = feat_width // 4
        for start in range(0, feat_width, band):
            value = contract(left[:, start : start + band], right, 0, 0).astype(jnp.bfloat16)
            for at in range(start, start + band, count):
                index = at // count
                y, x, z = (
                    index // (columns * owners),
                    index // owners % columns,
                    index % owners,
                )
                stage[y, x, z] = value[at - start : at - start + count]

    def middle_phase(parts, middle, cot_ref, dots_parts, dots_sum):
        loads = (
            pltpu.make_async_copy(dots_hbm, dots_parts, load_sem.at[0]),
            pltpu.make_async_copy(cot_hbm.at[mine], cot_ref, load_sem.at[3]),
            pltpu.make_async_copy(parts_hbm, parts, load_sem.at[1]),
            pltpu.make_async_copy(middle_hbm, middle, load_sem.at[2]),
        )
        for copy in loads:
            copy.start()
        for shift in range(owners):
            comb_load(shift).start()
        for copy in loads:
            copy.wait()
        small_sum[...] = jnp.zeros_like(small_sum)
        dots_sum[...] = sum(dots_parts[b] for b in range(owners)).T

        def body(step, carry):
            at = pl.ds(pl.multiple_of(step * tile, tile), tile)
            grad = sum(parts[b, at].astype(jnp.float32) for b in range(owners))
            gates = gates_ref[at]
            grad_gate = RESIDUAL * dots_sum[at]
            grad_logits = (
                gates * (grad_gate - jnp.sum(gates * grad_gate, axis=-1, keepdims=True))
            ).astype(jnp.bfloat16)
            grad = grad + contract(
                grad_logits[:, : router_ref.shape[0]], router_ref[...], 1, 0
            )
            unit, inv_rms = norm_parts(middle[at])
            expert_in = (unit * gains_ref[1:2]).astype(jnp.bfloat16)
            after = cot_ref[at].astype(jnp.float32) + norm_grad(
                grad, gains_ref[1:2], unit, inv_rms
            )
            grad_middle[at] = after
            to = pl.ds(pl.multiple_of(core * half + step * tile, tile), tile)
            grad_attn[to] = (RESIDUAL * after).astype(jnp.bfloat16)
            count = small_sum.shape[0]
            small_sum[...] += contract(grad_logits, expert_in, 0, 0)[:count]
            small_sum[count - 2 : count - 1] += jnp.sum(grad * unit, axis=0, keepdims=True)
            return carry

        lax.fori_loop(0, half // tile, body, 0)

    pl.run_scoped(
        middle_phase,
        pltpu.VMEM(parts_hbm.shape, parts_hbm.dtype),
        pltpu.VMEM(middle_hbm.shape, middle_hbm.dtype),
        pltpu.VMEM(middle_hbm.shape, cot_hbm.dtype),
        pltpu.VMEM(dots_hbm.shape, dots_hbm.dtype),
        pltpu.VMEM(gates_ref.shape, dots_hbm.dtype),
    )
    attn_swap = to_sibling(grad_attn.at[mine], grad_attn.at[mine], 0)
    attn_swap.start()
    for shift in range(owners):
        comb_load(shift).wait()
    comb_send_on(owners - 1)
    to_sibling(grad_attn.at[others], grad_attn.at[others], 0).wait_recv()

    causal = length // 2

    def attention_phase(
        out_weight_ref, heads_ref, query_ref, key_ref, value_ref, key_sum, value_sum, normed_ref
    ):
        load_normed = pltpu.make_async_copy(normed_hbm, normed_ref, load_sem.at[0])
        loads = (
            pltpu.make_async_copy(heads_hbm, heads_ref, load_sem.at[4]),
            pltpu.make_async_copy(out_weight_hbm, out_weight_ref, load_sem.at[5]),
            pltpu.make_async_copy(query_hbm, query_ref, load_sem.at[6]),
            pltpu.make_async_copy(key_hbm, key_ref, load_sem.at[7]),
            pltpu.make_async_copy(value_hbm, value_ref, load_sem.at[8]),
        )
        for copy in loads:
            copy.start()
        load_normed.start()
        loads[0].wait()
        cut = heads_ref.shape[1] // 2
        weight_grad(out_a, grad_attn, heads_ref[:, :cut])
        output_job_a.start(0)
        weight_grad(out_b, grad_attn, heads_ref[:, cut:])
        output_job_b.start(0)
        for copy in loads[1:]:
            copy.wait()

        def turned_back(grads):
            swapped = jnp.concatenate(
                [grads[:, head_size // 2 :], grads[:, : head_size // 2]], axis=1
            )
            return (grads * cosine_ref[...] + swapped * sine_ref[...]).astype(jnp.bfloat16)

        def body(group, carry):
            grad_heads = contract(grad_attn[...], out_weight_ref[group], 1, 1).astype(jnp.bfloat16)
            keys, values = key_ref[group], value_ref[group]
            key_sum[...] = jnp.zeros_like(key_sum)
            value_sum[...] = jnp.zeros_like(value_sum)
            turned = []
            for member in range(groups):
                query = query_ref[group * groups + member]
                grad_head = grad_heads[:, member * head_size : (member + 1) * head_size]
                pieces = []
                for start in (0, causal):
                    stop = start + causal
                    some_q, some_g = query[start:stop], grad_head[start:stop]
                    some_k, some_v = keys[:stop], values[:stop]
                    scores = contract(some_q, some_k, 1, 1) * ATTN_SCALE
                    row = start + lax.broadcasted_iota(jnp.int32, scores.shape, 0)
                    col = lax.broadcasted_iota(jnp.int32, scores.shape, 1)
                    scores = jnp.where(row >= col, scores, NEGATIVE)
                    raised = jnp.exp(scores - jnp.max(scores, axis=1, keepdims=True))
                    probs = raised * (1.0 / jnp.sum(raised, axis=1, keepdims=True))
                    grad_probs = contract(some_g, some_v, 1, 1)
                    value_sum[:stop] += contract(probs.astype(jnp.bfloat16), some_g, 0, 0)
                    grad_scores = (
                        probs
                        * (grad_probs - jnp.sum(probs * grad_probs, axis=1, keepdims=True))
                    ).astype(jnp.bfloat16)
                    pieces.append(
                        jnp.dot(grad_scores, some_k, preferred_element_type=jnp.float32)
                    )
                    key_sum[:stop] += contract(grad_scores, some_q, 0, 0)
                turned.append(turned_back(ATTN_SCALE * jnp.concatenate(pieces, axis=0)))
            grad_query[group] = jnp.concatenate(turned, axis=1)
            grad_keyvalue[0, group] = turned_back(ATTN_SCALE * key_sum[...])
            grad_keyvalue[1, group] = value_sum[...].astype(jnp.bfloat16)

            @pl.when(group < local)
            def _():
                first_sum(group)

            return carry

        pairs = kv_heads // 2
        for pair, (jobs, stages) in enumerate(zip(pair_jobs, pair_stages)):
            chosen = range(pair * pairs, (pair + 1) * pairs)
            lax.fori_loop(chosen[0], chosen[-1] + 1, body, 0)
            queries = jnp.concatenate([grad_query[g] for g in chosen], axis=1)
            keyvalue = jnp.concatenate(
                [grad_keyvalue[what, g] for what in range(2) for g in chosen], axis=1
            )
            if pair == 0:
                comb_stage(owners - 2)
                load_normed.wait()
            weight_grad(stages[0], normed_ref, queries)
            jobs[0].start(0)
            weight_grad(stages[1], normed_ref, keyvalue)
            jobs[1].start(0)
            if pair == 0:
                lax.fori_loop(held, local, start_first, 0)

    pl.run_scoped(
        attention_phase,
        pltpu.VMEM(out_weight_hbm.shape, out_weight_hbm.dtype),
        pltpu.VMEM(heads_hbm.shape, heads_hbm.dtype),
        pltpu.VMEM(query_hbm.shape, query_hbm.dtype),
        pltpu.VMEM(key_hbm.shape, key_hbm.dtype),
        pltpu.VMEM(value_hbm.shape, value_hbm.dtype),
        pltpu.VMEM((length, head_size), jnp.float32),
        pltpu.VMEM((length, head_size), jnp.float32),
        pltpu.VMEM(normed_hbm.shape, normed_hbm.dtype),
    )
    def start_second(expert, carry):
        for plan in plans:
            for copy in second_copies(plan, expert):
                copy.start()
            keep(plan, expert).start()
        return carry

    for which in pair_jobs[0]:
        which.forward(0)
    for away in range(owners - 3, 0, -1):
        comb_stage(away)

    def tokens_phase(query_weight, keyvalue_weight, grad_normed, tokens_ref):
        loads = (
            pltpu.make_async_copy(tokens_hbm.at[mine], tokens_ref, load_sem.at[3]),
            pltpu.make_async_copy(query_weight_hbm, query_weight, load_sem.at[1]),
            pltpu.make_async_copy(keyvalue_weight_hbm, keyvalue_weight, load_sem.at[2]),
        )
        for copy in loads:
            copy.start()
        queries = jnp.concatenate([grad_query[g] for g in range(kv_heads)], axis=1)
        keyvalue = [
            jnp.concatenate([grad_keyvalue[what, g] for g in range(kv_heads)], axis=1)
            for what in range(2)
        ]
        for copy in loads:
            copy.wait()
        grad_normed[...] = (
            contract(queries, query_weight[...], 1, 1)
            + contract(keyvalue[0], keyvalue_weight[0], 1, 1)
            + contract(keyvalue[1], keyvalue_weight[1], 1, 1)
        )
        half_send[...] = grad_normed[others].astype(jnp.bfloat16)
        swap = to_sibling(half_send, half_land, 1)
        swap.start()
        swap.wait_recv()

        def body(step, carry):
            at = pl.ds(pl.multiple_of(step * tile, tile), tile)
            to = pl.ds(pl.multiple_of(core * half + step * tile, tile), tile)
            grad = grad_normed[to] + half_land[at].astype(jnp.float32)
            unit, inv_rms = norm_parts(tokens_ref[at].astype(jnp.float32))
            grad_middle[at] += norm_grad(grad, gains_ref[0:1], unit, inv_rms)
            count = small_sum.shape[0]
            small_sum[count - 1 : count] += jnp.sum(grad * unit, axis=0, keepdims=True)
            return carry

        lax.fori_loop(0, half // tile, body, 0)

    pl.run_scoped(
        tokens_phase,
        pltpu.VMEM(query_weight_hbm.shape, query_weight_hbm.dtype),
        pltpu.VMEM(keyvalue_weight_hbm.shape, keyvalue_weight_hbm.dtype),
        pltpu.VMEM((2 * half, feat_width), jnp.float32),
        pltpu.VMEM((half, feat_width), tokens_hbm.dtype),
    )
    tokens_store = pltpu.make_async_copy(grad_middle, tokens_grad_hbm.at[mine], store_sem.at[0])
    tokens_store.start()
    tokens_swap = to_sibling(grad_middle, tokens_grad_hbm.at[mine], 2)
    tokens_swap.start()
    small_exchange = to_sibling(small_sum, small_swap, 3)
    small_exchange.start()

    small_exchange.wait()
    small_sum[...] += small_swap[...]
    piece = feat_width // (rows * columns * owners)
    small_stage[...] = jnp.zeros_like(small_stage)
    for y in range(rows):
        for x in range(columns):
            for z in range(owners):
                at = ((y * columns + x) * owners + z) * piece
                small_stage[y, x, z, :, :piece] = small_sum[:, at : at + piece]
    small_job.start(0)

    output_job_b.forward(0)
    for which in pair_jobs[1]:
        which.forward(0)
    for expert in range(kv_heads, local):
        first_sum(expert)
    lax.fori_loop(0, local, start_second, 0)
    for which in pair_jobs[0]:
        which.forward(1)
    output_job_a.forward(0)
    output_job_b.forward(1)
    for which in pair_jobs[1]:
        which.forward(1)
    output_job_a.forward(1)
    small_job.forward(0)
    small_job.forward(1)

    def mixed_phase(middle):
        load = pltpu.make_async_copy(middle_hbm, middle, load_sem.at[1])
        load.start()
        comb_stage(0)
        load.wait()

        def body(step, carry):
            at = pl.ds(pl.multiple_of(step * tile, tile), tile)
            comb = comb_own[0, at].astype(jnp.float32)
            mixed_stage[at] = (middle[at] + RESIDUAL * comb).astype(jnp.bfloat16)
            return carry

        lax.fori_loop(0, half // tile, body, 0)

    pl.run_scoped(mixed_phase, pltpu.VMEM(middle_hbm.shape, middle_hbm.dtype))
    mixed_store = pltpu.make_async_copy(mixed_stage, mixed_hbm.at[mine], store_sem.at[1])
    mixed_store.start()
    mixed_swap = to_sibling(mixed_stage, mixed_hbm.at[mine], 4)
    mixed_swap.start()

    cut = out_a.shape[4]
    output_out[:, :cut] = output_job_a.total(2)
    output_out[:, cut:] = output_job_b.total(2)
    small = small_job.total(2)
    count = small.shape[0]
    router_out[...] = small[: router_out.shape[0], :piece]
    expert_gain_out[...] = small[count - 2 : count - 1, :piece]
    attn_gain_out[...] = small[count - 1 :, :piece]
    for pair, jobs in enumerate(pair_jobs):
        cut = near_q.shape[4]
        query_out[:, pair * cut : (pair + 1) * cut] = jobs[0].total(2)
        value = jobs[1].total(2)
        cut = near_kv.shape[4] // 2
        for what in range(2):
            keyvalue_out[what, :, pair * cut : (pair + 1) * cut] = value[
                :, what * cut : (what + 1) * cut
            ]

    def close(expert, carry):
        for plan in plans:

            @pl.when(expert >= early)
            def _():
                for copy in first_copies(plan, expert):
                    copy.wait_send()

            for copy in second_copies(plan, expert):
                copy.wait()
            keep(plan, expert).wait()
        return carry

    lax.fori_loop(0, local, close, 0)
    for away in range(1, owners):
        for side in (1, -1):

            @pl.when(inside(me + side * away))
            def _():
                comb_copy(side, away).wait_send()

    for which in (output_job_a, output_job_b, small_job) + pair_jobs[0] + pair_jobs[1]:
        which.close()
    attn_swap.wait_send()
    to_sibling(half_send, half_land, 1).wait_send()
    tokens_store.wait()
    mixed_store.wait()
    tokens_swap.wait_send()
    mixed_swap.wait_send()
    to_sibling(grad_middle, tokens_grad_hbm.at[others], 2).wait_recv()
    to_sibling(mixed_stage, mixed_hbm.at[others], 4).wait_recv()


def backward(
    parts,
    dots,
    combs,
    grads,
    early_a,
    early_b,
    gates,
    middle,
    cot,
    tokens,
    gains,
    router,
    out_weight,
    heads_out,
    query,
    keys,
    values,
    normed,
    query_weight,
    keyvalue_weight,
    cosine,
    sine,
):
    owners = lax.axis_size("expert")
    chunks = lax.axis_size("dp")
    rows, columns = factors(chunks)
    half, feat_width = middle.shape
    local, _, height, units = grads.shape[2:]
    early = early_a.shape[1]
    piece = feat_width // (chunks * owners)
    heads, length, head_size = query.shape
    kv_heads = keys.shape[0]
    query_width, key_width = heads * head_size, kv_heads * head_size
    lanes = 128
    count = 24
    out_weight = out_weight.reshape(kv_heads, query_width // kv_heads, feat_width)
    bf16, f32 = jnp.bfloat16, jnp.float32
    hbm = pl.BlockSpec(memory_space=pl.ANY)
    vmem = pl.BlockSpec(memory_space=pltpu.VMEM)
    dma = pltpu.SemaphoreType.DMA
    most = max(rows, columns, owners) - 1

    def landings(tail, order, dtype):
        sizes = {"y": rows, "x": columns, "z": owners}
        left = ["y", "x", "z"]
        found = []
        for axis in order:
            left.remove(axis)
            found.append(
                pltpu.VMEM((sizes[axis] - 1,) + tuple(sizes[a] for a in left) + tail, dtype)
            )
        return found

    whole = (rows, columns, owners)
    return pl.pallas_call(
        functools.partial(back_kernel, rows, columns, owners),
        in_specs=[hbm] * 6 + [vmem] + [hbm] * 3 + [vmem] * 2 + [hbm] * 8 + [vmem, vmem],
        out_specs=[hbm] * 5 + [vmem] * 6,
        out_shape=[
            jax.ShapeDtypeStruct((2 * half, feat_width), bf16),
            jax.ShapeDtypeStruct((2 * half, feat_width), f32),
            jax.ShapeDtypeStruct((2, local, height, units), bf16),
            jax.ShapeDtypeStruct((rows - 1, local, height, units), bf16),
            jax.ShapeDtypeStruct((columns - 1, local, height, units), bf16),
            jax.ShapeDtypeStruct((piece, query_width), f32),
            jax.ShapeDtypeStruct((2, piece, key_width), f32),
            jax.ShapeDtypeStruct((piece, query_width), f32),
            jax.ShapeDtypeStruct((router.shape[0], piece), f32),
            jax.ShapeDtypeStruct((1, piece), f32),
            jax.ShapeDtypeStruct((1, piece), f32),
        ],
        scratch_shapes=[
            pltpu.VMEM((2, rows, height, units), bf16),
            pltpu.VMEM((2, columns, height, units), bf16),
            pltpu.VMEM((columns - 1, local, rows, height, units), bf16),
            pltpu.VMEM((rows - 1, local, columns, height, units), bf16),
            pltpu.VMEM((owners, half, feat_width), bf16),
            pltpu.VMEM((owners - 1, half, feat_width), bf16),
            pltpu.VMEM((owners - 1, half, feat_width), bf16),
            pltpu.VMEM(whole + (piece, query_width // 2), bf16),
            *landings((piece, query_width // 2), "zxy", bf16),
            pltpu.VMEM(whole + (piece, query_width // 2), bf16),
            *landings((piece, query_width // 2), "yxz", bf16),
            pltpu.VMEM(whole + (piece, query_width // 2), bf16),
            *landings((piece, query_width // 2), "xyz", bf16),
            pltpu.VMEM(whole + (piece, key_width), bf16),
            *landings((piece, key_width), "yxz", bf16),
            pltpu.VMEM(whole + (piece, query_width // 2), bf16),
            *landings((piece, query_width // 2), "yxz", bf16),
            pltpu.VMEM(whole + (piece, key_width), bf16),
            *landings((piece, key_width), "xyz", bf16),
            pltpu.VMEM((count, feat_width), f32),
            pltpu.VMEM((count, feat_width), f32),
            pltpu.VMEM(whole + (count, lanes), f32),
            *landings((count, lanes), "zxy", f32),
            pltpu.VMEM((2 * half, feat_width), bf16),
            pltpu.VMEM((half, feat_width), f32),
            pltpu.VMEM((kv_heads, length, query_width // kv_heads), bf16),
            pltpu.VMEM((2, kv_heads, length, head_size), bf16),
            pltpu.VMEM((half, feat_width), bf16),
            pltpu.VMEM((half, feat_width), bf16),
            pltpu.VMEM((half, feat_width), bf16),
            dma((9,)),
            dma((2, local)),
            dma((2, local)),
            dma((2, early)),
            dma((2, most, local)),
            dma((2, most, local)),
            dma((2, most, local)),
            dma((2, most, local)),
            dma((owners,)),
            dma((2, owners)),
            dma((2, owners)),
            dma((7, 3, most)),
            dma((7, 3, most)),
            dma((5,)),
            dma((5,)),
            dma((2,)),
        ],
        compiler_params=pltpu.CompilerParams(
            vmem_limit_bytes=60 * 2**20, collective_id=1, has_side_effects=True
        ),
        cost_estimate=pl.CostEstimate(
            flops=12 * 2**30, bytes_accessed=60 * 2**20, transcendentals=heads * length * length
        ),
    )(
        parts,
        dots,
        combs,
        grads,
        early_a,
        early_b,
        gates,
        middle,
        cot,
        tokens,
        gains,
        router,
        out_weight,
        heads_out,
        query,
        keys,
        values,
        normed,
        query_weight,
        keyvalue_weight,
        cosine,
        sine,
    )


def finish_body(large, kept_a, kept_b, second_a, second_b, *refs):
    count = (len(refs) - 4 - large) // 2
    sources, gateup_out, down_out = refs[:count], refs[count], refs[count + 1]
    targets, held = refs[count + 2 : 2 * count + 2], refs[2 * count + 2 : -2]
    load_sem, store_sem = refs[-2:]
    step = pl.program_id(0)
    steps = pl.num_programs(0)
    width = gateup_out.shape[2]
    loads = [
        pltpu.make_async_copy(sources[at], held[at], load_sem.at[at]) for at in range(large)
    ]
    stores = [
        pltpu.make_async_copy(held[at], targets[at], store_sem.at[at]) for at in range(large)
    ]

    @pl.when(step == 0)
    def _():
        for copy in loads:
            copy.start()
        for at in range(large, count):
            targets[at][...] = sources[at][...]

    @pl.when(step == 1)
    def _():
        for load, store in zip(loads, stores):
            load.wait()
            store.start()

    turned = []
    for part, (kept, second) in enumerate(((kept_a, second_a), (kept_b, second_b))):
        value = kept[0, 0].astype(jnp.float32)
        for other in range(second.shape[0]):
            value = value + second[other, 0].astype(jnp.float32)
        gateup_out[0, part] = value[:width]
        turned.append(value[width:])
    down_out[0] = jnp.concatenate(turned, axis=0).T

    @pl.when(step == steps - 1)
    def _():
        for copy in stores:
            copy.wait()


def finish(kept, second_a, second_b, *wholes):
    _, local, height, units = kept.shape
    width = 2 * height // 3
    large = 2
    spaces = [pl.BlockSpec(memory_space=pl.ANY)] * large
    spaces += [pl.BlockSpec(memory_space=pltpu.VMEM)] * (len(wholes) - large)

    def piece(count, at):
        return pl.BlockSpec((count, 1, height, units), lambda step: (at, step, 0, 0))

    return pl.pallas_call(
        functools.partial(finish_body, large),
        grid=(local,),
        in_specs=[
            piece(1, 0),
            piece(1, 1),
            piece(second_a.shape[0], 0),
            piece(second_b.shape[0], 0),
        ]
        + spaces,
        out_specs=[
            pl.BlockSpec((1, 2, width, units), lambda step: (step, 0, 0, 0)),
            pl.BlockSpec((1, units, width), lambda step: (step, 0, 0)),
        ]
        + spaces,
        out_shape=[
            jax.ShapeDtypeStruct((local, 2, width, units), jnp.float32),
            jax.ShapeDtypeStruct((local, units, width), jnp.float32),
        ]
        + [jax.ShapeDtypeStruct(w.shape, w.dtype) for w in wholes],
        scratch_shapes=[pltpu.VMEM(w.shape, w.dtype) for w in wholes[:large]]
        + [pltpu.SemaphoreType.DMA((large,)), pltpu.SemaphoreType.DMA((large,))],
        compiler_params=pltpu.CompilerParams(vmem_limit_bytes=60 * 2**20),
    )(kept, kept, second_a, second_b, *wholes)


def per_device(
    tokens,
    out_grad,
    attn_gain,
    query_weight,
    key_value_weight,
    output_weight,
    expert_gain,
    router_weight,
    gateup_weight,
    down_weight,
    routes,
):
    cosine, sine = rotary_tables()
    gains = jnp.stack([attn_gain, expert_gain])
    parts, dots, combs, gates, grads, early_a, early_b, _, _, normed, *kept = experts(
        tokens,
        out_grad,
        routes.T,
        gains,
        cosine,
        sine,
        router_weight.T,
        query_weight,
        key_value_weight,
        output_weight,
        gateup_weight,
        down_weight,
    )
    query, keys, values, heads_out, middle = kept
    mixed, tokens_grad, kept, second_a, second_b, *small = backward(
        parts,
        dots,
        combs,
        grads,
        early_a,
        early_b,
        gates,
        middle,
        out_grad,
        tokens,
        gains,
        router_weight.T,
        output_weight,
        heads_out,
        query,
        keys,
        values,
        normed,
        query_weight,
        key_value_weight,
        cosine,
        sine,
    )
    (
        gateup_total,
        down_total,
        mixed,
        tokens_grad,
        query_total,
        keyvalue_total,
        output_total,
        router_total,
        expert_gain_total,
        attn_gain_total,
    ) = finish(kept, second_a, second_b, mixed, tokens_grad, *small)
    return (
        mixed,
        tokens_grad,
        attn_gain_total[0],
        query_total,
        keyvalue_total,
        output_total.T,
        expert_gain_total[0],
        router_total.T,
        gateup_total,
        down_total,
    )


def solution(mesh):
    placed = (
        P(("dp", "expert"), None),
        P(("dp", "expert"), None),
        P(),
        P(None, "tensor"),
        P(None, None, "tensor"),
        P("tensor", None),
        P(),
        P(),
        P("expert", None, None, "tensor"),
        P("expert", "tensor", None),
        P(("dp", "expert"), None),
    )
    return jax.shard_map(
        per_device,
        mesh=mesh,
        in_specs=placed,
        out_specs=(
            P(("dp", "expert"), None),
            P(("dp", "expert"), None),
            P(("dp", "expert")),
            P(("dp", "expert"), "tensor"),
            P(None, ("dp", "expert"), "tensor"),
            P("tensor", ("dp", "expert")),
            P(("dp", "expert")),
            P(("dp", "expert"), None),
            P("expert", None, "dp", "tensor"),
            P("expert", "tensor", "dp"),
        ),
        check_vma=False,
    )
```

profile of v0, /device:TPU:15, one launch (start us, length us, event | category | flops | bytes accessed | tf_op | source)
XLA Modules:
  0.0 324.8 jit_solution(5536779457482846247)
XLA Ops:
  0.6 0.7 stack.9
  1.3 0.7 stack.10
  2.0 0.6 pad_maximum_fusion.gains_ref
  2.7 177.5 %shard_map.204 = (bf16[4,256,1536]{2,1,0:T(8,128)(2,1)}, f32[4,32,256]{2,1,0:T(8,128)}, bf16[4,256,1536]{2,1,0:T(8,128)(2,1)}, f32[256,32]{1,0:T(8,128)}, bf16[2...) custom-call(bf16[512,1536]{1,0:T(8,128)(2,1)} %tokens_hbm.3, ...), custom_call_target="tpu_custom_call" | custom-call | flops 72477573120 | bytes 83886080 | tf_op jit(solution)/shard_map/pallas_call | solution.py:944
  180.2 134.4 %shard_map.205 = (bf16[512,1536]{1,0:T(8,128)(2,1)}, f32[512,1536]{1,0:T(8,128)}, bf16[2,5,576,256]{3,2,1,0:T(8,128)(2,1)}, bf16[1,5,576,256]{3,2,1,0:T(8,128)(2...) custom-call(bf16[4,256,1536]{2,1,0:T(8,128)(2,1)} %get-tuple-element, ...), custom_call_target="tpu_custom_call" | custom-call | flops 12884901888 | bytes 62914560 | tf_op jit(solution)/shard_map/pallas_call | solution.py:1791
  314.5 9.8 %shard_map.206 = (f32[5,2,384,256]{3,2,1,0:T(8,128)}, f32[5,256,384]{2,1,0:T(8,128)}, bf16[512,1536]{1,0:T(8,128)(2,1)}, f32[512,1536]{1,0:T(8,128)}, f32[96,768...) custom-call(bf16[2,5,576,256]{3,2,1,0:T(8,128)(2,1)} %get-tuple-elem, ...), custom_call_target="tpu_custom_call" | custom-call | tf_op jit(solution)/shard_map/pallas_call | solution.py:1941
where the time goes:
time: 330 us; the launch traced here: 325 us
  Pallas kernels  322 us (98%)
    pallas_call x1, Pallas kernels, experts(): pl.pallas_call(functools.partial(expert_kernel, rows, columns, owners, lo...  177 us
    pallas_call x1, Pallas kernels, backward(): pl.pallas_call(functools.partial(back_kernel, rows, columns, owners), in_...  134 us
    pallas_call x1, Pallas kernels, finish(): pl.pallas_call(functools.partial(finish_body, large), grid=(local,), in_s...  9.78 us

commit v1 on v0

--- a/solution.py
+++ b/solution.py
@@ -1206,7 +1206,6 @@
             peers.append(place.device(axis, place.peer(axis, shift)))
     for peer in peers:
         pl.semaphore_signal(barrier, inc=1, device_id=peer, device_id_type=pl.DeviceIdType.MESH)
-    pl.semaphore_wait(barrier, len(peers))
 
     def to_sibling(src, dst, at):
         return pltpu.make_async_remote_copy(
@@ -1316,7 +1315,6 @@
         return carry
 
     held = local - 1
-    lax.fori_loop(early, held, start_first, 0)
     for plan in plans:
         for expert in range(early):
             early_load(plan, expert).start()
@@ -1423,6 +1421,8 @@
         )
         for copy in loads:
             copy.start()
+        pl.semaphore_wait(barrier, len(peers))
+        lax.fori_loop(early, held, start_first, 0)
         for shift in range(owners):
             comb_load(shift).start()
         for copy in loads:
@@ -1579,11 +1579,6 @@
             keep(plan, expert).start()
         return carry
 
-    for which in pair_jobs[0]:
-        which.forward(0)
-    for away in range(owners - 3, 0, -1):
-        comb_stage(away)
-
     def tokens_phase(query_weight, keyvalue_weight, grad_normed, tokens_ref):
         loads = (
             pltpu.make_async_copy(tokens_hbm.at[mine], tokens_ref, load_sem.at[3]),
@@ -1592,6 +1587,10 @@
         )
         for copy in loads:
             copy.start()
+        for which in pair_jobs[0]:
+            which.forward(0)
+        for away in range(owners - 3, 0, -1):
+            comb_stage(away)
         queries = jnp.concatenate([grad_query[g] for g in range(kv_heads)], axis=1)
         keyvalue = [
             jnp.concatenate([grad_keyvalue[what, g] for g in range(kv_heads)], axis=1)

time: 330 us -> 327 us (level)
  the two profiles are of different devices: /device:TPU:15 before, /device:TPU:0 now
where the time goes in v1:
time: 327 us; the launch traced here: 321 us
  Pallas kernels  318 us (97%)
    pallas_call x1, Pallas kernels, experts(): pl.pallas_call(functools.partial(expert_kernel, rows, columns, owners, lo...  178 us
    pallas_call x1, Pallas kernels, backward(): pl.pallas_call(functools.partial(back_kernel, rows, columns, owners), in_...  130 us
    pallas_call x1, Pallas kernels, finish(): pl.pallas_call(functools.partial(finish_body, large), grid=(local,), in_s...  9.78 us

profile of v1, /device:TPU:0, one launch (start us, length us, event | category | flops | bytes accessed | tf_op | source)
XLA Modules:
  0.0 321.0 jit_solution(3388998028072773270)
XLA Ops:
  0.6 0.7 stack.9
  1.3 0.7 stack.10
  2.0 0.6 pad_maximum_fusion.gains_ref
  2.7 178.3 %shard_map.204 = (bf16[4,256,1536]{2,1,0:T(8,128)(2,1)}, f32[4,32,256]{2,1,0:T(8,128)}, bf16[4,256,1536]{2,1,0:T(8,128)(2,1)}, f32[256,32]{1,0:T(8,128)}, bf16[2...) custom-call(bf16[512,1536]{1,0:T(8,128)(2,1)} %tokens_hbm.3, ...), custom_call_target="tpu_custom_call" | custom-call | flops 72477573120 | bytes 83886080 | tf_op jit(solution)/shard_map/pallas_call | solution.py:944
  181.0 129.8 %shard_map.205 = (bf16[512,1536]{1,0:T(8,128)(2,1)}, f32[512,1536]{1,0:T(8,128)}, bf16[2,5,576,256]{3,2,1,0:T(8,128)(2,1)}, bf16[1,5,576,256]{3,2,1,0:T(8,128)(2...) custom-call(bf16[4,256,1536]{2,1,0:T(8,128)(2,1)} %get-tuple-element, ...), custom_call_target="tpu_custom_call" | custom-call | flops 12884901888 | bytes 62914560 | tf_op jit(solution)/shard_map/pallas_call | solution.py:1790
  310.8 9.8 %shard_map.206 = (f32[5,2,384,256]{3,2,1,0:T(8,128)}, f32[5,256,384]{2,1,0:T(8,128)}, bf16[512,1536]{1,0:T(8,128)(2,1)}, f32[512,1536]{1,0:T(8,128)}, f32[96,768...) custom-call(bf16[2,5,576,256]{3,2,1,0:T(8,128)(2,1)} %get-tuple-elem, ...), custom_call_target="tpu_custom_call" | custom-call | tf_op jit(solution)/shard_map/pallas_call | solution.py:1940
